TPU v7x, 32 devices: a whole 2x2x4 slice. The times are simulated.
32 devices in a mesh: obj: 4 (over y, core), scan: 8 (over z, x).
Axes of the slice: x: 2, y: 2, z: 4, core: 2. Of those that a mesh axis runs over, the one named last changes fastest.
Arguments:
- object_slab: float32 [2, 2, 1536, 4096], P(None, None, 'obj', 'scan'), may hold values from -4 to 4
- probe_mode_stack: float32 [6, 2, 256, 256], replicated, may hold values from -2 to 2
- offsets: int32 [96, 2], P(('obj', 'scan')), may hold values from 0 to 3840, as said below
- measured: float32 [96, 256, 256], P(('obj', 'scan')), may hold values from 0.05 to 3
- counts: int32 [32], P(('obj', 'scan')), may hold values from 1 to 3, as said below
Outputs:
- new_object: float32 [2, 2, 1536, 4096], P(None, None, 'obj', 'scan')
- new_probe: float32 [6, 2, 256, 256], replicated
Inputs may be any that keep to these rules, and one draw needn't show every extreme that they name: `offsets`: rows 3 d to 3 d + 2 belong to device d (devices in the order obj, then scan). Each row gives the object row and column of a patch's top-left pixel; that pixel lies in the device's own tile of 384 x 512 pixels, and the whole 256 x 256 patch lies inside the object. Device d uses its first counts[d] position slots; the others are ignored.
All inputs are finite; a program needn't handle non-finite values.
Results may differ from a plain program's by a relative error of at most 0.008.
The roundings to bfloat16 on the way count: a program that leaves them out, or rounds other values in their place, can miss the bound.
Values sent between devices are 32-bit elements; how exact they have to be, the bound alone decides.
A program may use at most 128 MiB of HBM per device.

v0:
```python
import math

import jax
import jax.numpy as jnp
from jax import lax
from jax.sharding import PartitionSpec as P

chirp_scale = 24.0
probe_step = 0.15


def from_behind(array, axis, by):
    count = lax.axis_size(axis)
    pairs = [(i, i + by) for i in range(count) if 0 <= i + by < count]
    return lax.ppermute(array, axis, pairs)


def dft_table(pattern, sign_factor):
    indices = jnp.arange(pattern, dtype=jnp.int32)
    phases = indices[:, None] * indices[None, :] % pattern
    angles = phases.astype(jnp.float32) * (2.0 * math.pi / pattern)
    normalizer = 1.0 / math.sqrt(pattern)
    real_part = jnp.cos(angles) * normalizer
    imag_part = sign_factor * jnp.sin(angles) * normalizer
    row_real = jnp.stack([real_part, -imag_part], axis=1)
    row_imag = jnp.stack([imag_part, real_part], axis=1)
    return jnp.stack([row_real, row_imag], axis=0).astype(jnp.bfloat16)


def propagator(pattern):
    indices = jnp.arange(pattern, dtype=jnp.int32)
    freqs = ((indices + pattern // 2) % pattern - pattern // 2).astype(jnp.float32) / pattern
    phases = -math.pi * chirp_scale * (freqs[:, None] ** 2 + freqs[None, :] ** 2)
    return jnp.stack([jnp.cos(phases), jnp.sin(phases)], axis=0)


def transform(field_in, tables):
    half_done = jnp.einsum("dkcy,mcyx->mdkx", tables, field_in, preferred_element_type=jnp.float32)
    half_done = half_done.astype(jnp.bfloat16)
    return jnp.einsum("mcyx,dkcx->mdyk", half_done, tables, preferred_element_type=jnp.float32)


def complex_times(left_arr, right_arr):
    left_real, left_imag = (left_arr[..., 0, :, :], left_arr[..., 1, :, :])
    right_real, right_imag = (right_arr[..., 0, :, :], right_arr[..., 1, :, :])
    return jnp.stack(
        [
            left_real * right_real - left_imag * right_imag,
            left_real * right_imag + left_imag * right_real,
        ],
        axis=-3,
    )


def conjugate(values):
    return jnp.stack([values[..., 0, :, :], -values[..., 1, :, :]], axis=-3)


def position_updates(
    object_window,
    probe_mode_stack,
    measured_pattern,
    propagate_forward,
    propagate_backward,
    fresnel_kernel,
):
    layers = object_window.shape[0]
    wavefield = probe_mode_stack
    inputs = []
    exit_wave = wavefield
    for layer_index in range(layers):
        inputs.append(wavefield)
        exit_wave = complex_times(object_window[layer_index], wavefield)
        if layer_index < layers - 1:
            spectrum = transform(exit_wave.astype(jnp.bfloat16), propagate_forward)
            wavefield = transform(
                complex_times(fresnel_kernel, spectrum).astype(jnp.bfloat16), propagate_backward
            )
    detector_wavefront = transform(exit_wave.astype(jnp.bfloat16), propagate_forward)
    modal_intensity = jnp.sum(detector_wavefront[:, 0] ** 2 + detector_wavefront[:, 1] ** 2, axis=0)
    amplitude_residual = (
        (modal_intensity - measured_pattern)[None, None] * detector_wavefront
    ).astype(jnp.bfloat16)
    gradient = transform(amplitude_residual, propagate_backward)
    pieces = [None] * layers
    for layer_index in reversed(range(layers)):
        if layer_index < layers - 1:
            spectrum = transform(gradient.astype(jnp.bfloat16), propagate_forward)
            gradient = transform(
                complex_times(conjugate(fresnel_kernel), spectrum).astype(jnp.bfloat16),
                propagate_backward,
            )
        pieces[layer_index] = jnp.sum(
            complex_times(conjugate(inputs[layer_index]), gradient), axis=0
        )
        gradient = complex_times(conjugate(object_window[layer_index]), gradient)
    return (jnp.stack(pieces, axis=0), gradient)


def on_device(object_slab, probe_mode_stack, offsets, measured, counts):
    layers = object_slab.shape[0]
    tile_height = object_slab.shape[2]
    tile_width = object_slab.shape[3]
    pattern = probe_mode_stack.shape[-1]
    propagate_forward = dft_table(pattern, -1.0)
    propagate_backward = dft_table(pattern, 1.0)
    fresnel_kernel = propagator(pattern)
    right_rim = from_behind(object_slab[:, :, :, :pattern], "scan", -1)
    lower_rim = from_behind(object_slab[:, :, :pattern, :], "obj", -1)
    corner_half = from_behind(object_slab[:, :, :pattern, :pattern], "scan", -1)
    corner_rim = from_behind(corner_half, "obj", -1)
    upper_part = jnp.concatenate([object_slab, right_rim], axis=3)
    lower_part = jnp.concatenate([lower_rim, corner_rim], axis=3)
    extended = jnp.concatenate([upper_part, lower_part], axis=2)
    row_base = lax.axis_index("obj") * tile_height
    col_base = lax.axis_index("scan") * tile_width
    lamp_power = jnp.sum(probe_mode_stack[:, 0] ** 2 + probe_mode_stack[:, 1] ** 2, axis=0)
    zero_index = jnp.int32(0)

    def visit_slot(slot_index, state_now):
        grad_ext, light_ext, grad_probe = state_now
        row_start = offsets[slot_index, 0] - row_base
        col_start = offsets[slot_index, 1] - col_base
        corner_at = (zero_index, zero_index, row_start, col_start)
        object_window = lax.dynamic_slice(extended, corner_at, (layers, 2, pattern, pattern))
        object_update, probe_update = position_updates(
            object_window,
            probe_mode_stack,
            measured[slot_index],
            propagate_forward,
            propagate_backward,
            fresnel_kernel,
        )
        previous = lax.dynamic_slice(grad_ext, corner_at, (layers, 2, pattern, pattern))
        grad_ext = lax.dynamic_update_slice(grad_ext, previous + object_update, corner_at)
        previous_light = lax.dynamic_slice(light_ext, (row_start, col_start), (pattern, pattern))
        light_ext = lax.dynamic_update_slice(
            light_ext, previous_light + lamp_power, (row_start, col_start)
        )
        return (grad_ext, light_ext, grad_probe + probe_update)

    start_state = (
        jnp.zeros(extended.shape, jnp.float32),
        jnp.zeros(extended.shape[2:], jnp.float32),
        jnp.zeros(probe_mode_stack.shape, jnp.float32),
    )
    used_count = counts[0]
    grad_ext, light_ext, grad_probe = lax.fori_loop(0, used_count, visit_slot, start_state)
    from_left = from_behind(
        (grad_ext[:, :, :tile_height, tile_width:], light_ext[:tile_height, tile_width:]), "scan", 1
    )
    from_above = from_behind(
        (grad_ext[:, :, tile_height:, :tile_width], light_ext[tile_height:, :tile_width]), "obj", 1
    )
    corner_half = from_behind(
        (grad_ext[:, :, tile_height:, tile_width:], light_ext[tile_height:, tile_width:]), "scan", 1
    )
    from_corner = from_behind((corner_half[0], corner_half[1]), "obj", 1)
    grad_tile = grad_ext[:, :, :tile_height, :tile_width]
    grad_tile = grad_tile.at[:, :, :, :pattern].add(from_left[0])
    grad_tile = grad_tile.at[:, :, :pattern, :].add(from_above[0])
    grad_tile = grad_tile.at[:, :, :pattern, :pattern].add(from_corner[0])
    light_tile = light_ext[:tile_height, :tile_width]
    light_tile = light_tile.at[:, :pattern].add(from_left[1])
    light_tile = light_tile.at[:pattern, :].add(from_above[1])
    light_tile = light_tile.at[:pattern, :pattern].add(from_corner[1])
    new_object = object_slab - grad_tile / (light_tile + 1.0)
    summed = lax.psum(grad_probe, ("obj", "scan"))
    grad_scale = jnp.sqrt(jnp.mean(summed * summed) + 1e-06)
    new_probe = probe_mode_stack - probe_step * summed / grad_scale
    return (new_object, new_probe)


def solution(mesh):
    in_specs = (
        P(None, None, "obj", "scan"),
        P(),
        P(("obj", "scan"), None),
        P(("obj", "scan"), None, None),
        P(("obj", "scan")),
    )
    out_specs = (P(None, None, "obj", "scan"), P())
    return jax.shard_map(
        on_device, mesh=mesh, in_specs=in_specs, out_specs=out_specs, check_vma=False
    )
```

profile of v0, /device:TPU:0, one launch (start us, length us, event | category | flops | bytes accessed | tf_op | source)
XLA Modules:
  0.0 519.7 jit_solution(227979585133459418)
XLA Ops:
  18.1 19.7 %collective-permute-done.2 = f32[2,2,256,256]{3,2,1,0:T(8,128)} collective-permute-done((f32[2,2,256,256]{3,2,1,0:T(8,128)S(1)}, f32[2,2,256,256]{3,2,1,0:T(8,128)}, u32[]{:S(2)}, u32[]{:S(2)}) %collective-permute-start.2) | collective-permute-done | bytes 1048608 | tf_op jit(solution)/shard_map/ppermute | solution.py:15
  47.5 23.1 %collective-permute-done = f32[2,2,384,256]{3,2,1,0:T(8,128)} collective-permute-done((f32[2,2,384,256]{3,2,1,0:T(8,128)}, f32[2,2,384,256]{3,2,1,0:T(8,128)}, u32[]{:S(2)}, u32[]{:S(2)}) %collective-permute-start) | collective-permute-done | bytes 1572896 | tf_op jit(solution)/shard_map/ppermute | solution.py:15
  70.6 5.0 maximum_maximum_fusion
  75.6 3.8 broadcast_in_dim.6
  82.8 82.2 %while.26 = (s32[]{:T(128)}, f32[2,2,640,768]{3,2,1,0:T(8,128)}, f32[640,768]{1,0:T(8,128)}, f32[6,2,256,256]{3,2,1,0:T(8,128)}, s32[]{:T(128)}, /*index=5*/s32[...) while((s32[]{:T(128)}, f32[2,2,640,768]{3,2,1,0:T(8,128)}, ...), condition=%wide.region_5.6_spmd.clone.clone.clone, body=%wide.region_1.5_spmd.clone.clone.clone.sunk | while | flops 9715843072 | bytes 127665712 | solution.py:148
  104.5 5.2 convolution_bitcast_fusion.14
  113.8 5.7 %convolution_bitcast_fusion.15 = f32[6,2,256,256]{3,2,1,0:T(8,128)} fusion(f32[6,2,256,256]{3,2,1,0:T(8,128)} %convolution_bitcast_fusion.14, f32[256,256]{1,0:T(8,128)} %get-tuple-element.690, bf16[2,256,2,256]{3,1,2,0:T(8,128)(2,1)} %get-tuple-element.760), kind=kOutput, calls=%fused_computation.15.clone.1 | convolution fusion | flops 1612972032 | bytes 7077888 | tf_op jit(solution)/shard_map/while/body/mcyx,dkcx->mdyk/dot_general | solution.py:40
  119.5 4.1 subtract_convert_fusion.13
  124.7 3.5 convolution_bitcast_fusion.16
  130.8 5.3 %convolution_bitcast_fusion.17 = f32[6,2,256,256]{3,2,1,0:T(8,128)} fusion(bf16[6,1,256,256]{3,2,1,0:T(8,128)(2,1)} %get-tuple-element.697, bf16[6,1,256,256]{3,2,1,0:T(8,128)(2,1)} %get-tuple-element.698, bf16[2,256,2,256]{3,1,2,0:T(8,128)(2,1)} %get-tuple-element.760), kind=kOutput, calls=%fused_computation.13.clone.1 | convolution fusion | flops 1614544896 | bytes 5242880 | tf_op jit(solution)/shard_map/while/body/mcyx,dkcx->mdyk/dot_general | solution.py:40
  136.1 4.7 multiply_subtract_fusion.4
  144.6 11.0 %dynamic_update_slice.20 = f32[2,2,640,768]{3,2,1,0:T(8,128)} dynamic-update-slice(f32[2,2,640,768]{3,2,1,0:T(8,128)} %get-tuple-element.728, f32[2,2,256,256]{3,2,1,0:T(8,128)} %maximum_add_fusion.4, s32[]{:T(128)} %constant.238.clone.1..sunk, s32[]{:T(128)} %constant.238.clone.1..sunk, s32[]{:T(128)S(6)} %select_n.143, s32[]{:T(128)S(6)} %select_n.144) | dynamic-update-slice | bytes 2097156 | tf_op jit(solution)/shard_map/while/body/dynamic_update_slice | solution.py:135
  155.7 3.5 dynamic_update_slice.21
  159.2 4.9 maximum_add_fusion.5
  167.9 6.2 %collective-permute-start.4 = (f32[2,2,384,256]{3,2,1,0:T(8,128)}, f32[2,2,384,256]{3,2,1,0:T(8,128)}, u32[]{:S(2)}, u32[]{:S(2)}) collective-permute-start(f32[2,2,384,256]{3,2,1,0:T(8,128)} %slice.335), channel_id=1, source_target_pairs={{0,1},{1,2},{2,3},{3,4},{4,5},{5,6},{6,7},{8,9},{9,10},{10,11},{11... | collective-permute-start | bytes 4718600 | tf_op jit(solution)/shard_map/ppermute | solution.py:15
  177.1 167.8 %collective-permute-start.9 = (f32[256,512]{1,0:T(8,128)}, f32[256,512]{1,0:T(8,128)}, u32[]{:S(2)}, u32[]{:S(2)}) collective-permute-start(f32[256,512]{1,0:T(8,128)} %slice.344), channel_id=1, source_target_pairs={{0,8},{8,16},{16,24},{1,9},{9,17},{17,25},{2,10},{10,18},{18,26},{... | collective-permute-start | bytes 1572872 | tf_op jit(solution)/shard_map/ppermute | solution.py:15
  352.0 3.9 slice.333
  359.4 27.0 %collective-permute-start.5 = (f32[2,2,256,512]{3,2,1,0:T(8,128)}, f32[2,2,256,512]{3,2,1,0:T(8,128)}, u32[]{:S(2)}, u32[]{:S(2)}) collective-permute-start(f32[2,2,256,512]{3,2,1,0:T(8,128)} %slice.337), channel_id=1, source_target_pairs={{0,8},{8,16},{16,24},{1,9},{9,17},{17,25},{2,10},{10,18},{18,26},{... | collective-permute-start | bytes 6291464 | tf_op jit(solution)/shard_map/ppermute | solution.py:15
  386.4 14.2 %collective-permute-start.11 = (f32[256,256]{1,0:T(8,128)}, f32[256,256]{1,0:T(8,128)S(1)}, u32[]{:S(2)}, u32[]{:S(2)}) collective-permute-start(f32[256,256]{1,0:T(8,128)} %collective-permute-done.10), channel_id=1, source_target_pairs={{0,8},{8,16},{16,24},{1,9},{9,17},{17,25},{2,10},{10,18},{18,26},{... | collective-permute-start | bytes 786440 | tf_op jit(solution)/shard_map/ppermute | solution.py:15
  404.6 25.1 %collective-permute-start.7 = (f32[2,2,256,256]{3,2,1,0:T(8,128)}, f32[2,2,256,256]{3,2,1,0:T(8,128)}, u32[]{:S(2)}, u32[]{:S(2)}) collective-permute-start(f32[2,2,256,256]{3,2,1,0:T(8,128)} %collective-permute-done.6), channel_id=1, source_target_pairs={{0,8},{8,16},{16,24},{1,9},{9,17},{17,25},{2,10},{10,18},{18,26},{... | collective-permute-start | bytes 3145736 | tf_op jit(solution)/shard_map/ppermute | solution.py:15
  433.0 60.6 %all-reduce.2.cloned.1.call-done = f32[6,2,256,256]{3,2,1,0:T(8,128)} async-done(((f32[6,2,256,256]{3,2,1,0:T(8,128)}), f32[6,2,256,256]{3,2,1,0:T(8,128)}) %all-reduce.2.cloned.1.call-update) | async-done | bytes 3145744 | tf_op jit(solution)/shard_map/psum | solution.py:168
  497.6 4.0 divide_subtract_fusion
  501.6 4.3 constant_dynamic-update-slice_fusion.1
  508.4 4.4 divide_subtract_fusion.1
  (89 shorter events, 84.6 us)
Async XLA Ops:
  7.2 486.4 %all-reduce.2.cloned.1.call-start = ((), (), s32[]{:S(2)}) async-start(), calls=%async_computation | async-start | bytes 6291456 | tf_op jit(solution)/shard_map/psum | solution.py:168
  8.5 6.0 %copy-start.4 = (f32[2,2,384,512]{3,2,1,0:T(8,128)S(1)}, f32[2,2,384,512]{3,2,1,0:T(8,128)}, u32[]{:S(2)}) copy-start(f32[2,2,384,512]{3,2,1,0:T(8,128)} %param.19) | copy-start | bytes 9437188
  8.5 29.2 %collective-permute-start.2 = (f32[2,2,256,256]{3,2,1,0:T(8,128)S(1)}, f32[2,2,256,256]{3,2,1,0:T(8,128)}, u32[]{:S(2)}, u32[]{:S(2)}) collective-permute-start(f32[2,2,256,256]{3,2,1,0:T(8,128)S(1)} %slice.330), channel_id=1, source_target_pairs={{1,0},{2,1},{3,2},{4,3},{5,4},{6,5},{7,6},{9,8},{10,9},{11,10},{12... | collective-permute-start | bytes 3145736 | tf_op jit(solution)/shard_map/ppermute | solution.py:15
  13.2 57.4 %collective-permute-start.1 = (f32[2,2,256,512]{3,2,1,0:T(8,128)}, f32[2,2,256,512]{3,2,1,0:T(8,128)}, u32[]{:S(2)}, u32[]{:S(2)}) collective-permute-start(f32[2,2,256,512]{3,2,1,0:T(8,128)} %slice.329), channel_id=1, source_target_pairs={{8,0},{16,8},{24,16},{9,1},{17,9},{25,17},{10,2},{18,10},{26,18},{... | collective-permute-start | bytes 6291464 | tf_op jit(solution)/shard_map/ppermute | solution.py:15
  15.8 54.8 %collective-permute-start = (f32[2,2,384,256]{3,2,1,0:T(8,128)}, f32[2,2,384,256]{3,2,1,0:T(8,128)}, u32[]{:S(2)}, u32[]{:S(2)}) collective-permute-start(f32[2,2,384,256]{3,2,1,0:T(8,128)} %slice.328), channel_id=1, source_target_pairs={{1,0},{2,1},{3,2},{4,3},{5,4},{6,5},{7,6},{9,8},{10,9},{11,10},{12... | collective-permute-start | bytes 4718600 | tf_op jit(solution)/shard_map/ppermute | solution.py:15
  37.7 32.9 %collective-permute-start.3 = (f32[2,2,256,256]{3,2,1,0:T(8,128)}, f32[2,2,256,256]{3,2,1,0:T(8,128)}, u32[]{:S(2)}, u32[]{:S(2)}) collective-permute-start(f32[2,2,256,256]{3,2,1,0:T(8,128)} %collective-permute-done.2), channel_id=1, source_target_pairs={{8,0},{16,8},{24,16},{9,1},{17,9},{25,17},{10,2},{18,10},{26,18},{... | collective-permute-start | bytes 3145736 | tf_op jit(solution)/shard_map/ppermute | solution.py:15
  43.0 2.3 copy-start
  45.3 25.3 %copy-start.5 = (f32[2,2,384,512]{3,2,1,0:T(8,128)S(1)}, f32[2,2,384,512]{3,2,1,0:T(8,128)}, u32[]{:S(2)}) copy-start(f32[2,2,384,512]{3,2,1,0:T(8,128)} %param.19) | copy-start | bytes 9437188
  80.8 2.0 copy-start.12
  109.6 2.2 copy-start.10
  130.8 5.3 %copy-start.1 = (f32[6,2,256,256]{3,2,1,0:T(8,128)S(1)}, f32[6,2,256,256]{3,2,1,0:T(8,128)}, u32[]{:S(2)}) copy-start(f32[6,2,256,256]{3,2,1,0:T(8,128)} %get-tuple-element.794) | copy-start | bytes 9437188 | tf_op jit(solution)/shard_map/while
  144.6 11.1 %copy-start.7 = (f32[256,256]{1,0:T(8,128)S(1)}, f32[256,256]{1,0:T(8,128)}, u32[]{:S(2)}) copy-start(f32[256,256]{1,0:T(8,128)} %get-tuple-element.702) | copy-start | bytes 786436 | tf_op jit(solution)/shard_map/while
  165.0 9.1 %copy-start.8 = (f32[640,768]{1,0:T(8,128)S(1)}, f32[640,768]{1,0:T(8,128)}, u32[]{:S(2)}) copy-start(f32[640,768]{1,0:T(8,128)} %get-tuple-element.774) | copy-start | bytes 5898244
  167.9 261.8 %collective-permute-start.4 = (f32[2,2,384,256]{3,2,1,0:T(8,128)}, f32[2,2,384,256]{3,2,1,0:T(8,128)}, u32[]{:S(2)}, u32[]{:S(2)}) collective-permute-start(f32[2,2,384,256]{3,2,1,0:T(8,128)} %slice.335), channel_id=1, source_target_pairs={{0,1},{1,2},{2,3},{3,4},{4,5},{5,6},{6,7},{8,9},{9,10},{10,11},{11... | collective-permute-start | bytes 4718600 | tf_op jit(solution)/shard_map/ppermute | solution.py:15
  174.1 212.3 %collective-permute-start.8 = (f32[384,256]{1,0:T(8,128)S(1)}, f32[384,256]{1,0:T(8,128)}, u32[]{:S(2)}, u32[]{:S(2)}) collective-permute-start(f32[384,256]{1,0:T(8,128)S(1)} %slice.342), channel_id=1, source_target_pairs={{0,1},{1,2},{2,3},{3,4},{4,5},{5,6},{6,7},{8,9},{9,10},{10,11},{11... | collective-permute-start | bytes 1179656 | tf_op jit(solution)/shard_map/ppermute | solution.py:15
  177.1 225.2 %collective-permute-start.9 = (f32[256,512]{1,0:T(8,128)}, f32[256,512]{1,0:T(8,128)}, u32[]{:S(2)}, u32[]{:S(2)}) collective-permute-start(f32[256,512]{1,0:T(8,128)} %slice.344), channel_id=1, source_target_pairs={{0,8},{8,16},{16,24},{1,9},{9,17},{17,25},{2,10},{10,18},{18,26},{... | collective-permute-start | bytes 1572872 | tf_op jit(solution)/shard_map/ppermute | solution.py:15
  345.6 13.7 %collective-permute-start.10 = (f32[256,256]{1,0:T(8,128)}, f32[256,256]{1,0:T(8,128)}, u32[]{:S(2)}, u32[]{:S(2)}) collective-permute-start(f32[256,256]{1,0:T(8,128)} %slice.346), channel_id=1, source_target_pairs={{0,1},{1,2},{2,3},{3,4},{4,5},{5,6},{6,7},{8,9},{9,10},{10,11},{11... | collective-permute-start | bytes 786440 | tf_op jit(solution)/shard_map/ppermute | solution.py:15
  349.0 55.6 %collective-permute-start.6 = (f32[2,2,256,256]{3,2,1,0:T(8,128)S(1)}, f32[2,2,256,256]{3,2,1,0:T(8,128)}, u32[]{:S(2)}, u32[]{:S(2)}) collective-permute-start(f32[2,2,256,256]{3,2,1,0:T(8,128)S(1)} %slice.339), channel_id=1, source_target_pairs={{0,1},{1,2},{2,3},{3,4},{4,5},{5,6},{6,7},{8,9},{9,10},{10,11},{11... | collective-permute-start | bytes 3145736 | tf_op jit(solution)/shard_map/ppermute | solution.py:15
  355.9 3.4 copy-start.9
  359.4 142.2 %collective-permute-start.5 = (f32[2,2,256,512]{3,2,1,0:T(8,128)}, f32[2,2,256,512]{3,2,1,0:T(8,128)}, u32[]{:S(2)}, u32[]{:S(2)}) collective-permute-start(f32[2,2,256,512]{3,2,1,0:T(8,128)} %slice.337), channel_id=1, source_target_pairs={{0,8},{8,16},{16,24},{1,9},{9,17},{17,25},{2,10},{10,18},{18,26},{... | collective-permute-start | bytes 6291464 | tf_op jit(solution)/shard_map/ppermute | solution.py:15
  386.4 17.2 %collective-permute-start.11 = (f32[256,256]{1,0:T(8,128)}, f32[256,256]{1,0:T(8,128)S(1)}, u32[]{:S(2)}, u32[]{:S(2)}) collective-permute-start(f32[256,256]{1,0:T(8,128)} %collective-permute-done.10), channel_id=1, source_target_pairs={{0,8},{8,16},{16,24},{1,9},{9,17},{17,25},{2,10},{10,18},{18,26},{... | collective-permute-start | bytes 786440 | tf_op jit(solution)/shard_map/ppermute | solution.py:15
  404.6 101.3 %collective-permute-start.7 = (f32[2,2,256,256]{3,2,1,0:T(8,128)}, f32[2,2,256,256]{3,2,1,0:T(8,128)}, u32[]{:S(2)}, u32[]{:S(2)}) collective-permute-start(f32[2,2,256,256]{3,2,1,0:T(8,128)} %collective-permute-done.6), channel_id=1, source_target_pairs={{0,8},{8,16},{16,24},{1,9},{9,17},{17,25},{2,10},{10,18},{18,26},{... | collective-permute-start | bytes 3145736 | tf_op jit(solution)/shard_map/ppermute | solution.py:15
  501.6 6.9 %copy-start.11 = (f32[384,512]{1,0:T(8,128)S(1)}, f32[384,512]{1,0:T(8,128)}, u32[]{:S(2)}) copy-start(f32[384,512]{1,0:T(8,128)} %broadcast_add_fusion) | copy-start | bytes 2359300
  505.9 2.5 copy-start.6
  (2 other events, 2.7 us)
Sparse Core Ops, SparseCore 0:
  347.8 145.7 all-reduce.1
where the time goes:
time: 523 us; the launch traced here: 520 us
  starting transfers between devices  252 us (48%)
  waiting for transfers between devices  103 us (20%)
  other arithmetic  74.3 us (14%)
  local copies, waits for them, and re-layouts  45.3 us (9%)
  matrix products  26.6 us (5%)
  between operations  14.9 us (3%)
    ppermute x12, starting transfers between devices, from_behind(): return lax.ppermute(array, axis, pairs)  252 us
    psum x1, waiting for transfers between devices, on_device(): summed = lax.psum(grad_probe, ('obj', 'scan'))  60.6 us
    ppermute x12, waiting for transfers between devices, from_behind(): return lax.ppermute(array, axis, pairs)  42.8 us
    dot_general x6, matrix products, transform(): jnp.einsum('mcyx,dkcx->mdyk', half_done, tables, preferred_element_type=j...  26.6 us
    another operation x11, other arithmetic  18.3 us
    dynamic_update_slice x1, local copies, waits for them, and re-layouts, visit_slot(): lax.dynamic_update_slice(grad_ext, previous + object_update, corner_at)  11 us
  transfers between devices with their start and end apart: 13, of which 3 were waited for; matrix products, arithmetic and copies ran while one was open for 8% of the time, Pallas kernels for 0%

commit v1 on v0

v1 whole, which is shorter than its diff:
```python
import functools
import math

import jax
import jax.numpy as jnp
import numpy as np
from jax import lax
from jax.experimental import pallas as pl
from jax.experimental.pallas import tpu as pltpu
from jax.sharding import PartitionSpec as P

chirp_scale = 24.0
probe_step = 0.15
lanes = 128
sublanes = 8
vmem_bytes = 56 * 1024 * 1024


def from_behind(array, axis, by):
    count = lax.axis_size(axis)
    pairs = [(i, i + by) for i in range(count) if 0 <= i + by < count]
    return lax.ppermute(array, axis, pairs)


def dft_matrix(pattern, sign_factor):
    indices = np.arange(pattern)
    angles = (indices[:, None] * indices[None, :] % pattern) * (2.0 * math.pi / pattern)
    real_part = np.cos(angles) / math.sqrt(pattern)
    imag_part = sign_factor * np.sin(angles) / math.sqrt(pattern)
    upper = np.concatenate([real_part, -imag_part], axis=1)
    lower = np.concatenate([imag_part, real_part], axis=1)
    return jnp.asarray(np.concatenate([upper, lower], axis=0).astype(np.float32), jnp.bfloat16)


def propagator(pattern):
    indices = np.arange(pattern)
    freqs = ((indices + pattern // 2) % pattern - pattern // 2) / pattern
    phases = -math.pi * chirp_scale * (freqs[:, None] ** 2 + freqs[None, :] ** 2)
    return jnp.asarray(np.stack([np.cos(phases), np.sin(phases)], axis=0).astype(np.float32))


def aligned(row, col):
    row_base = pl.multiple_of(row // sublanes * sublanes, sublanes)
    col_base = pl.multiple_of(col // lanes * lanes, lanes)
    return row_base, col_base, row - row_base, col - col_base


def pad(array):
    array = jnp.concatenate([array, jnp.zeros((array.shape[0], lanes), jnp.float32)], axis=1)
    return jnp.concatenate([array, jnp.zeros((sublanes, array.shape[1]), jnp.float32)], axis=0)


def roll_down(array, rows, cols):
    return pltpu.roll(pltpu.roll(array, cols, 1), rows, 0)


def transform(real_part, imag_part, left, right):
    pattern = real_part.shape[0]
    stacked = jnp.concatenate([real_part.astype(jnp.bfloat16), imag_part.astype(jnp.bfloat16)], axis=0)
    half = jnp.dot(left, stacked, preferred_element_type=jnp.float32).astype(jnp.bfloat16)
    half = jnp.concatenate([half[:pattern], half[pattern:]], axis=1)
    full = jnp.dot(half, right, preferred_element_type=jnp.float32)
    return full[:, :pattern], full[:, pattern:]


def slots_kernel(
    corners, used, tile, right, lower, corner, probe, measured, table_f, table_b, fresnel,
    grad_tile, grad_right, grad_lower, grad_corner, grad_probe,
    ext, grad, window, waves, far, intensity, term, sems_in, sems_out,
):
    modes, _, pattern, _ = probe.shape
    layers = tile.shape[0]
    height, width = tile.shape[2], tile.shape[3]
    wide = pattern + lanes
    tall = pattern + sublanes

    def spots(buffer):
        return (
            buffer.at[:, :, pl.ds(0, height), pl.ds(0, width)],
            buffer.at[:, :, pl.ds(0, height), pl.ds(width, pattern)],
            buffer.at[:, :, pl.ds(height, pattern), pl.ds(0, width)],
            buffer.at[:, :, pl.ds(height, pattern), pl.ds(width, pattern)],
        )

    loads = [
        pltpu.make_async_copy(source, spot, sems_in.at[k])
        for k, (source, spot) in enumerate(zip((tile, right, lower, corner), spots(ext)))
    ]
    for load in loads:
        load.start()
    grad[...] = jnp.zeros_like(grad)
    grad_probe[...] = jnp.zeros_like(grad_probe)
    for load in loads:
        load.wait()

    @pl.loop(0, used[0])
    def _(slot):
        row = corners[slot, 0]
        col = corners[slot, 1]
        row_base, col_base, row_shift, col_shift = aligned(row, col)
        row_back = jnp.where(row_shift == 0, 0, tall - row_shift)
        col_back = jnp.where(col_shift == 0, 0, wide - col_shift)
        for layer in range(layers):
            for part in range(2):
                block = ext[layer, part, pl.ds(row_base, tall), pl.ds(col_base, wide)]
                window[layer, part] = roll_down(block, row_back, col_back)[:pattern, :pattern]
        intensity[...] = jnp.zeros_like(intensity)
        term[...] = jnp.zeros_like(term)

        @pl.loop(0, modes)
        def _(mode):
            wr, wi = probe[mode, 0], probe[mode, 1]
            for layer in range(layers):
                o_r, o_i = window[layer, 0], window[layer, 1]
                fr, fi = transform(o_r * wr - o_i * wi, o_r * wi + o_i * wr, table_f[...], table_b[...])
                if layer < layers - 1:
                    hr, hi = fresnel[0], fresnel[1]
                    wr, wi = transform(hr * fr - hi * fi, hr * fi + hi * fr, table_b[...], table_f[...])
                    waves[layer, mode, 0] = wr
                    waves[layer, mode, 1] = wi
            far[mode, 0] = fr
            far[mode, 1] = fi
            intensity[...] += fr * fr + fi * fi

        intensity[...] = intensity[...] - measured[slot]

        @pl.loop(0, modes)
        def _(mode):
            gain = intensity[...]
            gr, gi = transform(gain * far[mode, 0], gain * far[mode, 1], table_b[...], table_f[...])
            for layer in reversed(range(layers)):
                if layer < layers - 1:
                    sr, si = transform(gr, gi, table_f[...], table_b[...])
                    hr, hi = fresnel[0], fresnel[1]
                    gr, gi = transform(hr * sr + hi * si, hr * si - hi * sr, table_b[...], table_f[...])
                if layer == 0:
                    wr, wi = probe[mode, 0], probe[mode, 1]
                else:
                    wr, wi = waves[layer - 1, mode, 0], waves[layer - 1, mode, 1]
                term[layer, 0] += wr * gr + wi * gi
                term[layer, 1] += wr * gi - wi * gr
                o_r, o_i = window[layer, 0], window[layer, 1]
                gr, gi = o_r * gr + o_i * gi, o_r * gi - o_i * gr
            grad_probe[mode, 0] += gr
            grad_probe[mode, 1] += gi

        for layer in range(layers):
            for part in range(2):
                at = (layer, part, pl.ds(row_base, tall), pl.ds(col_base, wide))
                grad[at] = grad[at] + roll_down(pad(term[layer, part]), row_shift, col_shift)

    saves = [
        pltpu.make_async_copy(spot, target, sems_out.at[k])
        for k, (spot, target) in enumerate(
            zip(spots(grad), (grad_tile, grad_right, grad_lower, grad_corner))
        )
    ]
    for save in saves:
        save.start()
    for save in saves:
        save.wait()


def run_slots(corners, used, tile, right, lower, corner, probe, measured, table_f, table_b, fresnel):
    layers, _, height, width = tile.shape
    modes, _, pattern, _ = probe.shape
    smem = pl.BlockSpec(memory_space=pltpu.SMEM)
    vmem = pl.BlockSpec(memory_space=pltpu.VMEM)
    anyw = pl.BlockSpec(memory_space=pl.ANY)
    f32 = jnp.float32
    ext_shape = (layers, 2, height + pattern, width + pattern)
    return pl.pallas_call(
        slots_kernel,
        out_shape=(
            jax.ShapeDtypeStruct(tile.shape, f32),
            jax.ShapeDtypeStruct(right.shape, f32),
            jax.ShapeDtypeStruct(lower.shape, f32),
            jax.ShapeDtypeStruct(corner.shape, f32),
            jax.ShapeDtypeStruct(probe.shape, f32),
        ),
        in_specs=[smem, smem, anyw, anyw, anyw, anyw, vmem, vmem, vmem, vmem, vmem],
        out_specs=(anyw, anyw, anyw, anyw, vmem),
        scratch_shapes=[
            pltpu.VMEM(ext_shape, f32),
            pltpu.VMEM(ext_shape, f32),
            pltpu.VMEM((layers, 2, pattern, pattern), f32),
            pltpu.VMEM((layers - 1, modes, 2, pattern, pattern), f32),
            pltpu.VMEM((modes, 2, pattern, pattern), f32),
            pltpu.VMEM((pattern, pattern), f32),
            pltpu.VMEM((layers, 2, pattern, pattern), f32),
            pltpu.SemaphoreType.DMA((4,)),
            pltpu.SemaphoreType.DMA((4,)),
        ],
        compiler_params=pltpu.CompilerParams(vmem_limit_bytes=vmem_bytes),
        cost_estimate=pl.CostEstimate(flops=29_000_000_000, bytes_accessed=30_000_000, transcendentals=0),
    )(corners, used, tile, right, lower, corner, probe, measured, table_f, table_b, fresnel)


def light_kernel(height, width, slots, info, probe, light, canvas, power):
    modes, _, pattern, _ = probe.shape
    total = jnp.zeros((pattern, pattern), jnp.float32)
    for mode in range(modes):
        total = total + (probe[mode, 0] * probe[mode, 0] + probe[mode, 1] * probe[mode, 1])
    power[...] = pad(total)
    canvas[...] = jnp.zeros_like(canvas)
    for block in range(4):
        base = block * (2 * slots + 1)

        @pl.loop(0, info[base + 2 * slots])
        def _(slot):
            row = info[base + 2 * slot] + height
            col = info[base + 2 * slot + 1] + width
            row_base, col_base, row_shift, col_shift = aligned(row, col)
            at = (pl.ds(row_base, pattern + sublanes), pl.ds(col_base, pattern + lanes))
            canvas[at] = canvas[at] + roll_down(power[...], row_shift, col_shift)

    light[...] = canvas[height : 2 * height, width : 2 * width] + 1.0


def run_light(height, width, slots, info, probe):
    pattern = probe.shape[-1]
    return pl.pallas_call(
        functools.partial(light_kernel, height, width, slots),
        out_shape=jax.ShapeDtypeStruct((height, width), jnp.float32),
        in_specs=[pl.BlockSpec(memory_space=pltpu.SMEM), pl.BlockSpec(memory_space=pltpu.VMEM)],
        out_specs=pl.BlockSpec(memory_space=pltpu.VMEM),
        scratch_shapes=[
            pltpu.VMEM((2 * height + pattern, 2 * width + pattern), jnp.float32),
            pltpu.VMEM((pattern + sublanes, pattern + lanes), jnp.float32),
        ],
        compiler_params=pltpu.CompilerParams(vmem_limit_bytes=24 * 1024 * 1024),
        cost_estimate=pl.CostEstimate(flops=10_000_000, bytes_accessed=12_000_000, transcendentals=0),
    )(info, probe)


def final_kernel(tile, grad, left, above, light, out):
    pattern = left.shape[-1]
    grad[0, 0, :, :pattern] = grad[0, 0, :, :pattern] + left[0, 0]
    grad[0, 0, :pattern, :] = grad[0, 0, :pattern, :] + above[0, 0]
    out[0, 0] = tile[0, 0] - grad[0, 0] / light[...]


def run_final(tile, grad, left, above, light):
    layers, parts, height, width = tile.shape
    spec = lambda array: pl.BlockSpec((1, 1) + array.shape[2:], lambda i, j: (i, j, 0, 0))
    return pl.pallas_call(
        final_kernel,
        grid=(layers, parts),
        out_shape=jax.ShapeDtypeStruct(tile.shape, jnp.float32),
        in_specs=[spec(tile), spec(grad), spec(left), spec(above), pl.BlockSpec(light.shape, lambda i, j: (0, 0))],
        out_specs=spec(tile),
        compiler_params=pltpu.CompilerParams(vmem_limit_bytes=24 * 1024 * 1024),
        cost_estimate=pl.CostEstimate(flops=4_000_000, bytes_accessed=14_000_000, transcendentals=0),
    )(tile, grad, left, above, light)


def on_device(object_slab, probe_mode_stack, offsets, measured, counts):
    tile_height = object_slab.shape[2]
    tile_width = object_slab.shape[3]
    pattern = probe_mode_stack.shape[-1]
    slots = offsets.shape[0]
    table_f = dft_matrix(pattern, -1.0)
    table_b = dft_matrix(pattern, 1.0)
    fresnel = propagator(pattern)
    right_rim = from_behind(object_slab[:, :, :, :pattern], "scan", -1)
    lower_rim = from_behind(object_slab[:, :, :pattern, :], "obj", -1)
    corner_rim = from_behind(right_rim[:, :, :pattern, :], "obj", -1)
    base = jnp.stack([lax.axis_index("obj") * tile_height, lax.axis_index("scan") * tile_width])
    base = base.astype(jnp.int32)
    corners = offsets - base
    own_info = jnp.concatenate([offsets.reshape(-1), counts])
    left_info = from_behind(own_info, "scan", 1)
    row_info = jnp.concatenate([own_info, left_info])
    info = jnp.concatenate([row_info, from_behind(row_info, "obj", 1)])
    shifts = jnp.tile(jnp.concatenate([jnp.tile(base, slots), jnp.zeros((1,), jnp.int32)]), 4)
    light = run_light(tile_height, tile_width, slots, info - shifts, probe_mode_stack)
    grad_tile, grad_right, grad_lower, grad_corner, grad_probe = run_slots(
        corners, counts, object_slab, right_rim, lower_rim, corner_rim, probe_mode_stack,
        measured, table_f, table_b, fresnel,
    )
    corner_half = from_behind(grad_corner, "scan", 1)
    from_left = from_behind(grad_right, "scan", 1)
    grad_lower = grad_lower.at[:, :, :, :pattern].add(corner_half)
    from_above = from_behind(grad_lower, "obj", 1)
    new_object = run_final(object_slab, grad_tile, from_left, from_above, light)
    summed = lax.psum(grad_probe, ("obj", "scan"))
    grad_scale = jnp.sqrt(jnp.mean(summed * summed) + 1e-06)
    new_probe = probe_mode_stack - probe_step * summed / grad_scale
    return (new_object, new_probe)


def solution(mesh):
    in_specs = (
        P(None, None, "obj", "scan"),
        P(),
        P(("obj", "scan"), None),
        P(("obj", "scan"), None, None),
        P(("obj", "scan")),
    )
    out_specs = (P(None, None, "obj", "scan"), P())
    return jax.shard_map(
        on_device, mesh=mesh, in_specs=in_specs, out_specs=out_specs, check_vma=False
    )
```

time: 523 us -> 323 us (0.62)
  starting transfers between devices: 252 us -> 95.3 us
  other arithmetic: 74.3 us -> 11.1 us
  waiting for transfers between devices: 103 us -> 152 us
  Pallas kernels: 0 us -> 43 us
  local copies, waits for them, and re-layouts: 45.3 us -> 5.38 us
  matrix products: 26.6 us -> 0 us
    ppermute x12 -> x8, starting transfers between devices: 252 us -> 95.3 us  [from_behind(): return lax.ppermute(array, axis, pairs)]
    pallas_call x0 -> x3, Pallas kernels: none -> 43 us  [the longest x1 36.9 us: run_slots(): pl.pallas_call(slots_kernel, out_shape=(jax.ShapeDtypeStruct(tile.shape,...]
    ppermute x12 -> x8, waiting for transfers between devices: 42.8 us -> 81.5 us  [from_behind(): return lax.ppermute(array, axis, pairs)]
    dot_general x6 -> x0, matrix products: 26.6 us -> none  [transform(): jnp.einsum('mcyx,dkcx->mdyk', half_done, tables, preferred_element_type=j...]
    another operation x13 -> x1, other arithmetic: 19.4 us -> 0.08 us  [on_device(): jnp.stack([lax.axis_index('obj') * tile_height, lax.axis_index('scan') *...]
    dynamic_update_slice x2 -> x0, local copies, waits for them, and re-layouts: 14.6 us -> none  [the longest x1 11 us: visit_slot(): lax.dynamic_update_slice(grad_ext, previous + object_update, corner_at)]
    slice x9 -> x1, local copies, waits for them, and re-layouts: 14.5 us -> 0.07 us  [on_device(): corner_rim = from_behind(right_rim[:, :, :pattern, :], 'obj', -1)]
    sub x3 -> x2, other arithmetic: 11.2 us -> 0.68 us  [the longest x1 0.6 us: on_device(): corners = offsets - base]
  transfers between devices with their start and end apart: 13 -> 9, of which waited for: 3 -> 6; matrix products, arithmetic and copies ran while one was open for 8% -> 4% of each run, Pallas kernels for 0% -> 0%
where the time goes in v1:
time: 323 us; the launch traced here: 322 us
  waiting for transfers between devices  152 us (47%)
  starting transfers between devices  95.3 us (30%)
  Pallas kernels  43 us (13%)
  between operations  15.5 us (5%)
  other arithmetic  11.1 us (3%)
  local copies, waits for them, and re-layouts  5.38 us (2%)
    ppermute x8, starting transfers between devices, from_behind(): return lax.ppermute(array, axis, pairs)  95.3 us
    ppermute x8, waiting for transfers between devices, from_behind(): return lax.ppermute(array, axis, pairs)  81.5 us
    psum x1, waiting for transfers between devices, on_device(): summed = lax.psum(grad_probe, ('obj', 'scan'))  70 us
    pallas_call x1, Pallas kernels, run_slots(): pl.pallas_call(slots_kernel, out_shape=(jax.ShapeDtypeStruct(tile.shape,...  36.9 us
  transfers between devices with their start and end apart: 9, of which 6 were waited for; matrix products, arithmetic and copies ran while one was open for 4% of the time, Pallas kernels for 0%

profile of v1, /device:TPU:0, one launch (start us, length us, event | category | flops | bytes accessed | tf_op | source)
XLA Modules:
  0.0 321.9 jit_solution(15594344862436916577)
XLA Ops:
  7.2 1.7 slice.38
  8.9 1.3 collective-permute-start
  10.2 1.5 slice.39
  11.7 1.3 collective-permute-start.1
  13.0 35.1 %collective-permute-done.right = f32[2,2,384,256]{3,2,1,0:T(8,128)S(1)} collective-permute-done((f32[2,2,384,256]{3,2,1,0:T(8,128)S(1)}, f32[2,2,384,256]{3,2,1,0:T(8,128)S(1)}, u32[]{:S(2)}, u32[]{:S(2)}) %collective-permute-start) | collective-permute-done | bytes 1572896 | tf_op jit(solution)/shard_map/ppermute | solution.py:22
  48.2 1.3 collective-permute-start.2
  50.4 0.6 broadcast_subtract_fusion.corners
  51.0 1.9 collective-permute-done.2.corner
  52.9 36.9 %shard_map.95 = (f32[2,2,384,512]{3,2,1,0:T(8,128)}, f32[2,2,384,256]{3,2,1,0:T(8,128)}, f32[2,2,256,512]{3,2,1,0:T(8,128)}, f32[2,2,256,256]{3,2,1,0:T(8,128)}, f32[6,2,256,256]{3,2,1,0:T(8,128)}) custom-call(s32[3,2]{1,0:T(4,128)} %broadcast_subtract_fusion.corners, s32[1]{0:T(128)S(6)} %copy.16.used, f32[2,2,384,512]{3,2,1,0:T(8,128)} %tile.22, ...), custom_call_target="tpu_custom_call" | custom-call | flops 28999999488 | bytes 30000000 | tf_op jit(solution)/shard_map/pallas_call | solution.py:172
  89.8 5.6 %collective-permute-start.4 = (f32[2,2,256,256]{3,2,1,0:T(8,128)}, f32[2,2,256,256]{3,2,1,0:T(8,128)}, u32[]{:S(2)}, u32[]{:S(2)}) collective-permute-start(f32[2,2,256,256]{3,2,1,0:T(8,128)} %get-tuple-element.22), channel_id=1, source_target_pairs={{0,1},{1,2},{2,3},{3,4},{4,5},{5,6},{6,7},{8,9},{9,10},{10,11},{11... | collective-permute-start | bytes 3145736 | tf_op jit(solution)/shard_map/ppermute | solution.py:22
  95.4 11.6 %collective-permute-done.4 = f32[2,2,256,256]{3,2,1,0:T(8,128)} collective-permute-done((f32[2,2,256,256]{3,2,1,0:T(8,128)}, f32[2,2,256,256]{3,2,1,0:T(8,128)}, u32[]{:S(2)}, u32[]{:S(2)}) %collective-permute-start.4) | collective-permute-done | bytes 1048608 | tf_op jit(solution)/shard_map/ppermute | solution.py:22
  107.0 2.7 add_dynamic-update-slice_fusion
  109.7 72.4 %collective-permute-start.5 = (f32[2,2,256,512]{3,2,1,0:T(8,128)}, f32[2,2,256,512]{3,2,1,0:T(8,128)}, u32[]{:S(2)}, u32[]{:S(2)}) collective-permute-start(f32[2,2,256,512]{3,2,1,0:T(8,128)} %add_dynamic-update-slice_fusion), channel_id=1, source_target_pairs={{0,8},{8,16},{16,24},{1,9},{9,17},{17,25},{2,10},{10,18},{18,26},{... | collective-permute-start | bytes 6291464 | tf_op jit(solution)/shard_map/ppermute | solution.py:22
  182.2 7.7 %collective-permute-start.3 = (f32[2,2,384,256]{3,2,1,0:T(8,128)}, f32[2,2,384,256]{3,2,1,0:T(8,128)}, u32[]{:S(2)}, u32[]{:S(2)}) collective-permute-start(f32[2,2,384,256]{3,2,1,0:T(8,128)} %get-tuple-element.20), channel_id=1, source_target_pairs={{0,1},{1,2},{2,3},{3,4},{4,5},{5,6},{6,7},{8,9},{9,10},{10,11},{11... | collective-permute-start | bytes 4718600 | tf_op jit(solution)/shard_map/ppermute | solution.py:22
  190.0 3.9 %collective-permute-start.6 = (s32[7]{0:T(128)S(1)}, s32[7]{0:T(128)S(1)}, u32[]{:S(2)}, u32[]{:S(2)}) collective-permute-start(s32[7]{0:T(128)S(1)} %pad_add_fusion.1), channel_id=1, source_target_pairs={{0,1},{1,2},{2,3},{3,4},{4,5},{5,6},{6,7},{8,9},{9,10},{10,11},{11... | collective-permute-start | bytes 92 | tf_op jit(solution)/shard_map/ppermute | solution.py:22
  194.1 32.2 %collective-permute-done.6 = s32[7]{0:T(128)S(1)} collective-permute-done((s32[7]{0:T(128)S(1)}, s32[7]{0:T(128)S(1)}, u32[]{:S(2)}, u32[]{:S(2)}) %collective-permute-start.6) | collective-permute-done | bytes 60 | tf_op jit(solution)/shard_map/ppermute | solution.py:22
  226.3 1.8 collective-permute-start.7
  228.2 0.7 collective-permute-done.7
  229.0 1.5 shard_map.96.light
  230.5 0.9 copy-done.4
  231.4 70.0 %all-reduce.2.cloned.1.call-done = f32[6,2,256,256]{3,2,1,0:T(8,128)} async-done(((f32[6,2,256,256]{3,2,1,0:T(8,128)}), f32[6,2,256,256]{3,2,1,0:T(8,128)}) %all-reduce.2.cloned.1.call-update) | async-done | bytes 3145744 | tf_op jit(solution)/shard_map/psum | solution.py:286
  301.5 3.3 %multiply_reduce_fusion = f32[]{:T(128)} fusion(f32[6,2,256,256]{3,2,1,0:T(8,128)} %all-reduce.2.cloned.1.call-done), kind=kLoop, calls=%fused_computation.1 | loop fusion | flops 1572863 | bytes 3145732 | tf_op jit(solution)/shard_map/reduce_sum | solution.py:287
  305.5 4.1 %divide_subtract_fusion = f32[6,2,256,256]{3,2,1,0:T(8,128)} fusion(f32[6,2,256,256]{3,2,1,0:T(8,128)S(1)} %copy-done.2, f32[6,2,256,256]{3,2,1,0:T(8,128)} %all-reduce.2.cloned.1.call-done, f32[]{:T(128)S(6)} %sqrt.3), kind=kLoop, calls=%fused_computation | loop fusion | flops 2359296 | bytes 9437188 | tf_op jit(solution)/shard_map/sub | solution.py:288
  310.5 4.6 %shard_map.97 = f32[2,2,384,512]{3,2,1,0:T(8,128)} custom-call(f32[2,2,384,512]{3,2,1,0:T(8,128)S(1)} %copy-done.1, f32[2,2,384,512]{3,2,1,0:T(8,128)S(1)} %copy-done.3, f32[2,2,384,256]{3,2,1,0:T(8,128)} %collective-permute-done.3.left, f32[2,2,256,512]{3,2,1,0:T(8,128)} %collective-permute-done.5.above, f32[384,512]{1,0:T(8,128)S(1)} %copy-done.5), custom_call_target="tpu_custom_call" | custom-call | flops 4000000 | bytes 14000000 | tf_op jit(solution)/shard_map/pallas_call | solution.py:246
  (34 shorter events, 1.8 us)
Async XLA Ops:
  7.2 3.0 copy-start
  7.2 294.3 %all-reduce.2.cloned.1.call-start = ((), (), s32[]{:S(2)}) async-start(), calls=%async_computation | async-start | bytes 6291456 | tf_op jit(solution)/shard_map/psum | solution.py:286
  8.9 40.6 %copy-start.7 = (s32[3,2]{0,1:T(2,128)S(1)}, s32[3,2]{0,1:T(2,128)}, u32[]{:S(2)}) copy-start(s32[3,2]{0,1:T(2,128)} %param.12) | copy-start | bytes 76
  8.9 39.2 %collective-permute-start = (f32[2,2,384,256]{3,2,1,0:T(8,128)S(1)}, f32[2,2,384,256]{3,2,1,0:T(8,128)S(1)}, u32[]{:S(2)}, u32[]{:S(2)}) collective-permute-start(f32[2,2,384,256]{3,2,1,0:T(8,128)S(1)} %slice.38), channel_id=1, source_target_pairs={{1,0},{2,1},{3,2},{4,3},{5,4},{6,5},{7,6},{9,8},{10,9},{11,10},{12... | collective-permute-start | bytes 4718600 | tf_op jit(solution)/shard_map/ppermute | solution.py:22
  11.7 39.3 %collective-permute-start.1 = (f32[2,2,256,512]{3,2,1,0:T(8,128)}, f32[2,2,256,512]{3,2,1,0:T(8,128)S(1)}, u32[]{:S(2)}, u32[]{:S(2)}) collective-permute-start(f32[2,2,256,512]{3,2,1,0:T(8,128)} %slice.39), channel_id=1, source_target_pairs={{8,0},{16,8},{24,16},{9,1},{17,9},{25,17},{10,2},{18,10},{26,18},{... | collective-permute-start | bytes 6291464 | tf_op jit(solution)/shard_map/ppermute | solution.py:22
  48.1 1.4 copy-start.6
  48.2 4.7 %collective-permute-start.2 = (f32[2,2,256,256]{3,2,1,0:T(8,128)S(1)}, f32[2,2,256,256]{3,2,1,0:T(8,128)}, u32[]{:S(2)}, u32[]{:S(2)}) collective-permute-start(f32[2,2,256,256]{3,2,1,0:T(8,128)S(1)} %slice.42), channel_id=1, source_target_pairs={{8,0},{16,8},{24,16},{9,1},{17,9},{25,17},{10,2},{18,10},{26,18},{... | collective-permute-start | bytes 3145736 | tf_op jit(solution)/shard_map/ppermute | solution.py:22
  51.0 1.9 copy-start.8
  89.8 17.2 %collective-permute-start.4 = (f32[2,2,256,256]{3,2,1,0:T(8,128)}, f32[2,2,256,256]{3,2,1,0:T(8,128)}, u32[]{:S(2)}, u32[]{:S(2)}) collective-permute-start(f32[2,2,256,256]{3,2,1,0:T(8,128)} %get-tuple-element.22), channel_id=1, source_target_pairs={{0,1},{1,2},{2,3},{3,4},{4,5},{5,6},{6,7},{8,9},{9,10},{10,11},{11... | collective-permute-start | bytes 3145736 | tf_op jit(solution)/shard_map/ppermute | solution.py:22
  95.4 133.6 %copy-start.2 = (f32[6,2,256,256]{3,2,1,0:T(8,128)S(1)}, f32[6,2,256,256]{3,2,1,0:T(8,128)}, u32[]{:S(2)}) copy-start(f32[6,2,256,256]{3,2,1,0:T(8,128)} %probe.3) | copy-start | bytes 9437188
  109.7 199.9 %collective-permute-start.5 = (f32[2,2,256,512]{3,2,1,0:T(8,128)}, f32[2,2,256,512]{3,2,1,0:T(8,128)}, u32[]{:S(2)}, u32[]{:S(2)}) collective-permute-start(f32[2,2,256,512]{3,2,1,0:T(8,128)} %add_dynamic-update-slice_fusion), channel_id=1, source_target_pairs={{0,8},{8,16},{16,24},{1,9},{9,17},{17,25},{2,10},{10,18},{18,26},{... | collective-permute-start | bytes 6291464 | tf_op jit(solution)/shard_map/ppermute | solution.py:22
  182.2 127.5 %collective-permute-start.3 = (f32[2,2,384,256]{3,2,1,0:T(8,128)}, f32[2,2,384,256]{3,2,1,0:T(8,128)}, u32[]{:S(2)}, u32[]{:S(2)}) collective-permute-start(f32[2,2,384,256]{3,2,1,0:T(8,128)} %get-tuple-element.20), channel_id=1, source_target_pairs={{0,1},{1,2},{2,3},{3,4},{4,5},{5,6},{6,7},{8,9},{9,10},{10,11},{11... | collective-permute-start | bytes 4718600 | tf_op jit(solution)/shard_map/ppermute | solution.py:22
  190.0 36.2 %collective-permute-start.6 = (s32[7]{0:T(128)S(1)}, s32[7]{0:T(128)S(1)}, u32[]{:S(2)}, u32[]{:S(2)}) collective-permute-start(s32[7]{0:T(128)S(1)} %pad_add_fusion.1), channel_id=1, source_target_pairs={{0,1},{1,2},{2,3},{3,4},{4,5},{5,6},{6,7},{8,9},{9,10},{10,11},{11... | collective-permute-start | bytes 92 | tf_op jit(solution)/shard_map/ppermute | solution.py:22
  226.3 2.6 collective-permute-start.7
  230.5 0.9 copy-start.4
  305.4 4.2 %copy-start.1 = (f32[2,2,384,512]{3,2,1,0:T(8,128)S(1)}, f32[2,2,384,512]{3,2,1,0:T(8,128)}, u32[]{:S(2)}) copy-start(f32[2,2,384,512]{3,2,1,0:T(8,128)} %tile.22) | copy-start | bytes 9437188
  305.5 4.5 %copy-start.3 = (f32[2,2,384,512]{3,2,1,0:T(8,128)S(1)}, f32[2,2,384,512]{3,2,1,0:T(8,128)}, u32[]{:S(2)}) copy-start(f32[2,2,384,512]{3,2,1,0:T(8,128)} %get-tuple-element.19.grad) | copy-start | bytes 9437188
  305.5 5.0 %copy-start.5 = (f32[384,512]{1,0:T(8,128)S(1)}, f32[384,512]{1,0:T(8,128)}, u32[]{:S(2)}) copy-start(f32[384,512]{1,0:T(8,128)} %copy-done.4) | copy-start | bytes 2359300
Sparse Core Ops, SparseCore 0:
  95.6 205.8 all-reduce.1

commit v2 on v1

--- a/solution.py
+++ b/solution.py
@@ -107,7 +107,7 @@
         intensity[...] = jnp.zeros_like(intensity)
         term[...] = jnp.zeros_like(term)
 
-        @pl.loop(0, modes)
+        @pl.loop(0, modes, unroll=2)
         def _(mode):
             wr, wi = probe[mode, 0], probe[mode, 1]
             for layer in range(layers):
@@ -124,7 +124,7 @@
 
         intensity[...] = intensity[...] - measured[slot]
 
-        @pl.loop(0, modes)
+        @pl.loop(0, modes, unroll=2)
         def _(mode):
             gain = intensity[...]
             gr, gi = transform(gain * far[mode, 0], gain * far[mode, 1], table_b[...], table_f[...])
@@ -233,25 +233,29 @@
     )(info, probe)
 
 
-def final_kernel(tile, grad, left, above, light, out):
+def final_kernel(tile, grad, left, above, corner, light, out):
     pattern = left.shape[-1]
     grad[0, 0, :, :pattern] = grad[0, 0, :, :pattern] + left[0, 0]
     grad[0, 0, :pattern, :] = grad[0, 0, :pattern, :] + above[0, 0]
+    grad[0, 0, :pattern, :pattern] = grad[0, 0, :pattern, :pattern] + corner[0, 0]
     out[0, 0] = tile[0, 0] - grad[0, 0] / light[...]
 
 
-def run_final(tile, grad, left, above, light):
+def run_final(tile, grad, left, above, corner, light):
     layers, parts, height, width = tile.shape
     spec = lambda array: pl.BlockSpec((1, 1) + array.shape[2:], lambda i, j: (i, j, 0, 0))
     return pl.pallas_call(
         final_kernel,
         grid=(layers, parts),
         out_shape=jax.ShapeDtypeStruct(tile.shape, jnp.float32),
-        in_specs=[spec(tile), spec(grad), spec(left), spec(above), pl.BlockSpec(light.shape, lambda i, j: (0, 0))],
+        in_specs=[
+            spec(tile), spec(grad), spec(left), spec(above), spec(corner),
+            pl.BlockSpec(light.shape, lambda i, j: (0, 0)),
+        ],
         out_specs=spec(tile),
         compiler_params=pltpu.CompilerParams(vmem_limit_bytes=24 * 1024 * 1024),
         cost_estimate=pl.CostEstimate(flops=4_000_000, bytes_accessed=14_000_000, transcendentals=0),
-    )(tile, grad, left, above, light)
+    )(tile, grad, left, above, corner, light)
 
 
 def on_device(object_slab, probe_mode_stack, offsets, measured, counts):
@@ -272,18 +276,22 @@
     left_info = from_behind(own_info, "scan", 1)
     row_info = jnp.concatenate([own_info, left_info])
     info = jnp.concatenate([row_info, from_behind(row_info, "obj", 1)])
+    right_rim, lower_rim, corner_rim, corners, info = lax.optimization_barrier(
+        (right_rim, lower_rim, corner_rim, corners, info)
+    )
     shifts = jnp.tile(jnp.concatenate([jnp.tile(base, slots), jnp.zeros((1,), jnp.int32)]), 4)
     light = run_light(tile_height, tile_width, slots, info - shifts, probe_mode_stack)
     grad_tile, grad_right, grad_lower, grad_corner, grad_probe = run_slots(
         corners, counts, object_slab, right_rim, lower_rim, corner_rim, probe_mode_stack,
         measured, table_f, table_b, fresnel,
     )
-    corner_half = from_behind(grad_corner, "scan", 1)
+    summed = lax.psum(grad_probe, ("obj", "scan"))
+    corner_half = from_behind(grad_corner, "obj", 1)
+    from_above = from_behind(grad_lower, "obj", 1)
     from_left = from_behind(grad_right, "scan", 1)
-    grad_lower = grad_lower.at[:, :, :, :pattern].add(corner_half)
-    from_above = from_behind(grad_lower, "obj", 1)
-    new_object = run_final(object_slab, grad_tile, from_left, from_above, light)
-    summed = lax.psum(grad_probe, ("obj", "scan"))
+    from_corner = from_behind(corner_half, "scan", 1)
+    new_object = run_final(object_slab, grad_tile, from_left, from_above, from_corner, light)
+    summed, new_object = lax.optimization_barrier((summed, new_object))
     grad_scale = jnp.sqrt(jnp.mean(summed * summed) + 1e-06)
     new_probe = probe_mode_stack - probe_step * summed / grad_scale
     return (new_object, new_probe)

time: 323 us -> 320 us (level)
  starting transfers between devices: 95.3 us -> 53.4 us
  Pallas kernels: 43 us -> 65.4 us
  waiting for transfers between devices: 152 us -> 169 us
    ppermute x8 -> x9, starting transfers between devices: 95.3 us -> 53.4 us  [from_behind(): return lax.ppermute(array, axis, pairs)]
    psum x1, waiting for transfers between devices: 70 us -> 108 us  [on_device(): summed = lax.psum(grad_probe, ('obj', 'scan'))]
    pallas_call x1, Pallas kernels: 36.9 us -> 58.7 us  [run_slots(): pl.pallas_call(slots_kernel, out_shape=(jax.ShapeDtypeStruct(tile.shape,...]
    ppermute x8 -> x9, waiting for transfers between devices: 81.5 us -> 61 us  [from_behind(): return lax.ppermute(array, axis, pairs)]
  transfers between devices with their start and end apart: 9 -> 10, of which waited for: 6 -> 5; matrix products, arithmetic and copies ran while one was open for 4% -> 1% of each run, Pallas kernels for 0% -> 2%
where the time goes in v2:
time: 320 us
  waiting for transfers between devices  169 us (53%)
  Pallas kernels  65.4 us (20%)
  starting transfers between devices  53.4 us (17%)
  between operations  15.5 us (5%)
  other arithmetic  8.25 us (3%)
  local copies, waits for them, and re-layouts  7.64 us (2%)
    psum x1, waiting for transfers between devices, on_device(): summed = lax.psum(grad_probe, ('obj', 'scan'))  108 us
    ppermute x9, waiting for transfers between devices, from_behind(): return lax.ppermute(array, axis, pairs)  61 us
    pallas_call x1, Pallas kernels, run_slots(): pl.pallas_call(slots_kernel, out_shape=(jax.ShapeDtypeStruct(tile.shape,...  58.7 us
    ppermute x9, starting transfers between devices, from_behind(): return lax.ppermute(array, axis, pairs)  53.4 us
  transfers between devices with their start and end apart: 10, of which 5 were waited for; matrix products, arithmetic and copies ran while one was open for 1% of the time, Pallas kernels for 2%

profile of v2, /device:TPU:0, one launch (start us, length us, event | category | flops | bytes accessed | tf_op | source)
XLA Modules:
  0.0 319.6 jit_solution(4756519436662767817)
XLA Ops:
  7.2 1.7 slice.9
  8.9 1.3 collective-permute-start
  10.2 1.5 slice.10
  11.7 1.3 collective-permute-start.1
  13.0 35.1 %collective-permute-done.right = f32[2,2,384,256]{3,2,1,0:T(8,128)S(1)} collective-permute-done((f32[2,2,384,256]{3,2,1,0:T(8,128)S(1)}, f32[2,2,384,256]{3,2,1,0:T(8,128)S(1)}, u32[]{:S(2)}, u32[]{:S(2)}) %collective-permute-start) | collective-permute-done | bytes 1572896 | tf_op jit(solution)/shard_map/ppermute | solution.py:22
  48.1 1.2 copy-done.5
  49.4 1.3 collective-permute-start.2
  51.6 4.5 %collective-permute-start.3 = (s32[7]{0:T(128)S(1)}, s32[7]{0:T(128)S(1)}, u32[]{:S(2)}, u32[]{:S(2)}) collective-permute-start(s32[7]{0:T(128)S(1)} %pad_add_fusion.1), channel_id=1, source_target_pairs={{0,1},{1,2},{2,3},{3,4},{4,5},{5,6},{6,7},{8,9},{9,10},{10,11},{11... | collective-permute-start | bytes 92 | tf_op jit(solution)/shard_map/ppermute | solution.py:22
  56.2 1.2 collective-permute-done.3
  57.5 2.2 collective-permute-start.4
  59.7 0.6 broadcast_subtract_fusion.corners
  60.6 1.0 copy-done.7
  61.5 58.7 %shard_map.95 = (f32[2,2,384,512]{3,2,1,0:T(8,128)}, f32[2,2,384,256]{3,2,1,0:T(8,128)}, f32[2,2,256,512]{3,2,1,0:T(8,128)}, f32[2,2,256,256]{3,2,1,0:T(8,128)}, f32[6,2,256,256]{3,2,1,0:T(8,128)}) custom-call(s32[3,2]{1,0:T(4,128)} %broadcast_subtract_fusion.corners, s32[1]{0:T(128)S(6)} %copy.15.used, f32[2,2,384,512]{3,2,1,0:T(8,128)} %tile.22, ...), custom_call_target="tpu_custom_call" | custom-call | flops 28999999488 | bytes 30000000 | tf_op jit(solution)/shard_map/pallas_call | solution.py:172
  120.2 2.3 collective-permute-start.7
  122.6 2.6 collective-permute-start.6
  125.2 11.2 %collective-permute-start.5 = (f32[2,2,384,256]{3,2,1,0:T(8,128)}, f32[2,2,384,256]{3,2,1,0:T(8,128)}, u32[]{:S(2)}, u32[]{:S(2)}) collective-permute-start(f32[2,2,384,256]{3,2,1,0:T(8,128)} %get-tuple-element.20), channel_id=1, source_target_pairs={{0,1},{1,2},{2,3},{3,4},{4,5},{5,6},{6,7},{8,9},{9,10},{10,11},{11... | collective-permute-start | bytes 4718600 | tf_op jit(solution)/shard_map/ppermute | solution.py:22
  136.4 26.7 %collective-permute-start.8 = (f32[2,2,256,256]{3,2,1,0:T(8,128)}, f32[2,2,256,256]{3,2,1,0:T(8,128)}, u32[]{:S(2)}, u32[]{:S(2)}) collective-permute-start(f32[2,2,256,256]{3,2,1,0:T(8,128)} %collective-permute-done.7), channel_id=1, source_target_pairs={{0,1},{1,2},{2,3},{3,4},{4,5},{5,6},{6,7},{8,9},{9,10},{10,11},{11... | collective-permute-start | bytes 3145736 | tf_op jit(solution)/shard_map/ppermute | solution.py:22
  163.4 1.9 copy-done.2
  165.3 1.9 shard_map.96.light
  167.2 24.5 %collective-permute-done.8.corner = f32[2,2,256,256]{3,2,1,0:T(8,128)} collective-permute-done((f32[2,2,256,256]{3,2,1,0:T(8,128)}, f32[2,2,256,256]{3,2,1,0:T(8,128)}, u32[]{:S(2)}, u32[]{:S(2)}) %collective-permute-start.8) | collective-permute-done | bytes 1048608 | tf_op jit(solution)/shard_map/ppermute | solution.py:22
  191.7 4.8 %shard_map.97 = f32[2,2,384,512]{3,2,1,0:T(8,128)} custom-call(f32[2,2,384,512]{3,2,1,0:T(8,128)S(1)} %copy-done.1, f32[2,2,384,512]{3,2,1,0:T(8,128)S(1)} %copy-done.4, f32[2,2,384,256]{3,2,1,0:T(8,128)} %collective-permute-done.5.left, f32[2,2,256,512]{3,2,1,0:T(8,128)} %collective-permute-done.6.above, f32[2,2,256,256]{3,2,1,0:T(8,128)} %collective-permute-done.8.corner, ...), custom_call_target="tpu_custom_call" | custom-call | flops 4000000 | bytes 14000000 | tf_op jit(solution)/shard_map/pallas_call | solution.py:247
  196.5 108.3 %all-reduce.2.cloned.1.call-done = f32[6,2,256,256]{3,2,1,0:T(8,128)} async-done(((f32[6,2,256,256]{3,2,1,0:T(8,128)}), f32[6,2,256,256]{3,2,1,0:T(8,128)}) %all-reduce.2.cloned.1.call-update) | async-done | bytes 3145744 | tf_op jit(solution)/shard_map/psum | solution.py:288
  304.8 3.3 %multiply_reduce_fusion = f32[]{:T(128)} fusion(f32[6,2,256,256]{3,2,1,0:T(8,128)} %all-reduce.2.cloned.1.call-done), kind=kLoop, calls=%fused_computation.1 | loop fusion | flops 1572863 | bytes 3145732 | tf_op jit(solution)/shard_map/reduce_sum | solution.py:295
  308.8 4.0 %divide_subtract_fusion = f32[6,2,256,256]{3,2,1,0:T(8,128)} fusion(f32[6,2,256,256]{3,2,1,0:T(8,128)S(1)} %copy-done.3, f32[6,2,256,256]{3,2,1,0:T(8,128)} %all-reduce.2.cloned.1.call-done, f32[]{:T(128)S(6)} %sqrt.3), kind=kLoop, calls=%fused_computation | loop fusion | flops 2359296 | bytes 9437188 | tf_op jit(solution)/shard_map/sub | solution.py:296
  (34 shorter events, 1.1 us)
Async XLA Ops:
  7.2 3.0 copy-start
  7.2 297.6 %all-reduce.2.cloned.1.call-start = ((), (), s32[]{:S(2)}) async-start(), calls=%async_computation | async-start | bytes 6291456 | tf_op jit(solution)/shard_map/psum | solution.py:288
  8.9 41.8 %copy-start.6 = (s32[3,2]{0,1:T(2,128)S(1)}, s32[3,2]{0,1:T(2,128)}, u32[]{:S(2)}) copy-start(s32[3,2]{0,1:T(2,128)} %param.10) | copy-start | bytes 76
  8.9 39.2 %collective-permute-start = (f32[2,2,384,256]{3,2,1,0:T(8,128)S(1)}, f32[2,2,384,256]{3,2,1,0:T(8,128)S(1)}, u32[]{:S(2)}, u32[]{:S(2)}) collective-permute-start(f32[2,2,384,256]{3,2,1,0:T(8,128)S(1)} %slice.9), channel_id=1, source_target_pairs={{1,0},{2,1},{3,2},{4,3},{5,4},{6,5},{7,6},{9,8},{10,9},{11,10},{12... | collective-permute-start | bytes 4718600 | tf_op jit(solution)/shard_map/ppermute | solution.py:22
  11.7 48.9 %collective-permute-start.1 = (f32[2,2,256,512]{3,2,1,0:T(8,128)}, f32[2,2,256,512]{3,2,1,0:T(8,128)}, u32[]{:S(2)}, u32[]{:S(2)}) collective-permute-start(f32[2,2,256,512]{3,2,1,0:T(8,128)} %slice.10), channel_id=1, source_target_pairs={{8,0},{16,8},{24,16},{9,1},{17,9},{25,17},{10,2},{18,10},{26,18},{... | collective-permute-start | bytes 6291464 | tf_op jit(solution)/shard_map/ppermute | solution.py:22
  48.1 1.2 copy-start.5
  49.4 11.2 %collective-permute-start.2 = (f32[2,2,256,256]{3,2,1,0:T(8,128)S(1)}, f32[2,2,256,256]{3,2,1,0:T(8,128)S(1)}, u32[]{:S(2)}, u32[]{:S(2)}) collective-permute-start(f32[2,2,256,256]{3,2,1,0:T(8,128)S(1)} %slice.12), channel_id=1, source_target_pairs={{8,0},{16,8},{24,16},{9,1},{17,9},{25,17},{10,2},{18,10},{26,18},{... | collective-permute-start | bytes 3145736 | tf_op jit(solution)/shard_map/ppermute | solution.py:22
  51.6 5.8 %collective-permute-start.3 = (s32[7]{0:T(128)S(1)}, s32[7]{0:T(128)S(1)}, u32[]{:S(2)}, u32[]{:S(2)}) collective-permute-start(s32[7]{0:T(128)S(1)} %pad_add_fusion.1), channel_id=1, source_target_pairs={{0,1},{1,2},{2,3},{3,4},{4,5},{5,6},{6,7},{8,9},{9,10},{10,11},{11... | collective-permute-start | bytes 92 | tf_op jit(solution)/shard_map/ppermute | solution.py:22
  57.5 3.0 collective-permute-start.4
  60.6 1.0 copy-start.7
  120.2 16.2 %collective-permute-start.7 = (f32[2,2,256,256]{3,2,1,0:T(8,128)}, f32[2,2,256,256]{3,2,1,0:T(8,128)}, u32[]{:S(2)}, u32[]{:S(2)}) collective-permute-start(f32[2,2,256,256]{3,2,1,0:T(8,128)} %get-tuple-element.22), channel_id=1, source_target_pairs={{0,8},{8,16},{16,24},{1,9},{9,17},{17,25},{2,10},{10,18},{18,26},{... | collective-permute-start | bytes 3145736 | tf_op jit(solution)/shard_map/ppermute | solution.py:22
  122.6 44.6 %collective-permute-start.6 = (f32[2,2,256,512]{3,2,1,0:T(8,128)}, f32[2,2,256,512]{3,2,1,0:T(8,128)}, u32[]{:S(2)}, u32[]{:S(2)}) collective-permute-start(f32[2,2,256,512]{3,2,1,0:T(8,128)} %get-tuple-element.21), channel_id=1, source_target_pairs={{0,8},{8,16},{16,24},{1,9},{9,17},{17,25},{2,10},{10,18},{18,26},{... | collective-permute-start | bytes 6291464 | tf_op jit(solution)/shard_map/ppermute | solution.py:22
  125.2 42.0 %collective-permute-start.5 = (f32[2,2,384,256]{3,2,1,0:T(8,128)}, f32[2,2,384,256]{3,2,1,0:T(8,128)}, u32[]{:S(2)}, u32[]{:S(2)}) collective-permute-start(f32[2,2,384,256]{3,2,1,0:T(8,128)} %get-tuple-element.20), channel_id=1, source_target_pairs={{0,1},{1,2},{2,3},{3,4},{4,5},{5,6},{6,7},{8,9},{9,10},{10,11},{11... | collective-permute-start | bytes 4718600 | tf_op jit(solution)/shard_map/ppermute | solution.py:22
  136.4 55.3 %copy-start.1 = (f32[2,2,384,512]{3,2,1,0:T(8,128)S(1)}, f32[2,2,384,512]{3,2,1,0:T(8,128)}, u32[]{:S(2)}) copy-start(f32[2,2,384,512]{3,2,1,0:T(8,128)} %tile.22) | copy-start | bytes 9437188
  136.4 55.3 %collective-permute-start.8 = (f32[2,2,256,256]{3,2,1,0:T(8,128)}, f32[2,2,256,256]{3,2,1,0:T(8,128)}, u32[]{:S(2)}, u32[]{:S(2)}) collective-permute-start(f32[2,2,256,256]{3,2,1,0:T(8,128)} %collective-permute-done.7), channel_id=1, source_target_pairs={{0,1},{1,2},{2,3},{3,4},{4,5},{5,6},{6,7},{8,9},{9,10},{10,11},{11... | collective-permute-start | bytes 3145736 | tf_op jit(solution)/shard_map/ppermute | solution.py:22
  163.4 1.9 copy-start.2
  165.3 26.4 %copy-start.4 = (f32[2,2,384,512]{3,2,1,0:T(8,128)S(1)}, f32[2,2,384,512]{3,2,1,0:T(8,128)}, u32[]{:S(2)}) copy-start(f32[2,2,384,512]{3,2,1,0:T(8,128)} %get-tuple-element.19.grad) | copy-start | bytes 9437188
  196.5 112.3 %copy-start.3 = (f32[6,2,256,256]{3,2,1,0:T(8,128)S(1)}, f32[6,2,256,256]{3,2,1,0:T(8,128)}, u32[]{:S(2)}) copy-start(f32[6,2,256,256]{3,2,1,0:T(8,128)} %probe.3) | copy-start | bytes 9437188
Sparse Core Ops, SparseCore 0:
  136.5 168.2 all-reduce.1

commit v3 on v2

--- a/solution.py
+++ b/solution.py
@@ -233,15 +233,14 @@
     )(info, probe)
 
 
-def final_kernel(tile, grad, left, above, corner, light, out):
+def final_kernel(tile, grad, left, above, light, out):
     pattern = left.shape[-1]
     grad[0, 0, :, :pattern] = grad[0, 0, :, :pattern] + left[0, 0]
     grad[0, 0, :pattern, :] = grad[0, 0, :pattern, :] + above[0, 0]
-    grad[0, 0, :pattern, :pattern] = grad[0, 0, :pattern, :pattern] + corner[0, 0]
     out[0, 0] = tile[0, 0] - grad[0, 0] / light[...]
 
 
-def run_final(tile, grad, left, above, corner, light):
+def run_final(tile, grad, left, above, light):
     layers, parts, height, width = tile.shape
     spec = lambda array: pl.BlockSpec((1, 1) + array.shape[2:], lambda i, j: (i, j, 0, 0))
     return pl.pallas_call(
@@ -249,13 +248,13 @@
         grid=(layers, parts),
         out_shape=jax.ShapeDtypeStruct(tile.shape, jnp.float32),
         in_specs=[
-            spec(tile), spec(grad), spec(left), spec(above), spec(corner),
+            spec(tile), spec(grad), spec(left), spec(above),
             pl.BlockSpec(light.shape, lambda i, j: (0, 0)),
         ],
         out_specs=spec(tile),
         compiler_params=pltpu.CompilerParams(vmem_limit_bytes=24 * 1024 * 1024),
         cost_estimate=pl.CostEstimate(flops=4_000_000, bytes_accessed=14_000_000, transcendentals=0),
-    )(tile, grad, left, above, corner, light)
+    )(tile, grad, left, above, light)
 
 
 def on_device(object_slab, probe_mode_stack, offsets, measured, counts):
@@ -288,9 +287,9 @@
     summed = lax.psum(grad_probe, ("obj", "scan"))
     corner_half = from_behind(grad_corner, "obj", 1)
     from_above = from_behind(grad_lower, "obj", 1)
+    grad_right = grad_right.at[:, :, :pattern, :].add(corner_half)
     from_left = from_behind(grad_right, "scan", 1)
-    from_corner = from_behind(corner_half, "scan", 1)
-    new_object = run_final(object_slab, grad_tile, from_left, from_above, from_corner, light)
+    new_object = run_final(object_slab, grad_tile, from_left, from_above, light)
     summed, new_object = lax.optimization_barrier((summed, new_object))
     grad_scale = jnp.sqrt(jnp.mean(summed * summed) + 1e-06)
     new_probe = probe_mode_stack - probe_step * summed / grad_scale

time: 320 us -> 327 us (1.022)
  waiting for transfers between devices: 169 us -> 176 us
  starting transfers between devices: 53.4 us -> 50.1 us
    ppermute x9 -> x8, waiting for transfers between devices: 61 us -> 64.7 us  [from_behind(): return lax.ppermute(array, axis, pairs)]
    psum x1, waiting for transfers between devices: 108 us -> 112 us  [on_device(): summed = lax.psum(grad_probe, ('obj', 'scan'))]
    ppermute x9 -> x8, starting transfers between devices: 53.4 us -> 50.1 us  [from_behind(): return lax.ppermute(array, axis, pairs)]
  transfers between devices with their start and end apart: 10 -> 9, of which waited for: 5 -> 5; matrix products, arithmetic and copies ran while one was open for 1% -> 2% of each run, Pallas kernels for 2% -> 2%
where the time goes in v3:
time: 327 us; the launch traced here: 326 us
  waiting for transfers between devices  176 us (54%)
  Pallas kernels  65.1 us (20%)
  starting transfers between devices  50.1 us (15%)
  between operations  15.5 us (5%)
  other arithmetic  10.6 us (3%)
  local copies, waits for them, and re-layouts  7.81 us (2%)
    psum x1, waiting for transfers between devices, on_device(): summed = lax.psum(grad_probe, ('obj', 'scan'))  112 us
    ppermute x8, waiting for transfers between devices, from_behind(): return lax.ppermute(array, axis, pairs)  64.7 us
    pallas_call x1, Pallas kernels, run_slots(): pl.pallas_call(slots_kernel, out_shape=(jax.ShapeDtypeStruct(tile.shape,...  58.7 us
    ppermute x8, starting transfers between devices, from_behind(): return lax.ppermute(array, axis, pairs)  50.1 us
  transfers between devices with their start and end apart: 9, of which 5 were waited for; matrix products, arithmetic and copies ran while one was open for 2% of the time, Pallas kernels for 2%

profile of v3, /device:TPU:0, one launch (start us, length us, event | category | flops | bytes accessed | tf_op | source)
XLA Modules:
  0.0 325.7 jit_solution(12875368509874228292)
XLA Ops:
  7.2 1.7 slice.38
  8.9 1.3 collective-permute-start
  10.2 1.5 slice.39
  11.7 1.3 collective-permute-start.1
  13.0 35.1 %collective-permute-done.right = f32[2,2,384,256]{3,2,1,0:T(8,128)S(1)} collective-permute-done((f32[2,2,384,256]{3,2,1,0:T(8,128)S(1)}, f32[2,2,384,256]{3,2,1,0:T(8,128)S(1)}, u32[]{:S(2)}, u32[]{:S(2)}) %collective-permute-start) | collective-permute-done | bytes 1572896 | tf_op jit(solution)/shard_map/ppermute | solution.py:22
  48.1 1.2 copy-done.5
  49.4 1.3 collective-permute-start.2
  51.6 4.5 %collective-permute-start.3 = (s32[7]{0:T(128)S(1)}, s32[7]{0:T(128)S(1)}, u32[]{:S(2)}, u32[]{:S(2)}) collective-permute-start(s32[7]{0:T(128)S(1)} %pad_add_fusion.1), channel_id=1, source_target_pairs={{0,1},{1,2},{2,3},{3,4},{4,5},{5,6},{6,7},{8,9},{9,10},{10,11},{11... | collective-permute-start | bytes 92 | tf_op jit(solution)/shard_map/ppermute | solution.py:22
  56.2 1.2 collective-permute-done.3
  57.5 2.2 collective-permute-start.4
  59.7 0.6 broadcast_subtract_fusion.corners
  60.6 1.0 copy-done.7
  61.5 58.7 %shard_map.95 = (f32[2,2,384,512]{3,2,1,0:T(8,128)}, f32[2,2,384,256]{3,2,1,0:T(8,128)}, f32[2,2,256,512]{3,2,1,0:T(8,128)}, f32[2,2,256,256]{3,2,1,0:T(8,128)}, f32[6,2,256,256]{3,2,1,0:T(8,128)}) custom-call(s32[3,2]{1,0:T(4,128)} %broadcast_subtract_fusion.corners, s32[1]{0:T(128)S(6)} %copy.16.used, f32[2,2,384,512]{3,2,1,0:T(8,128)} %tile.22, ...), custom_call_target="tpu_custom_call" | custom-call | flops 28999999488 | bytes 30000000 | tf_op jit(solution)/shard_map/pallas_call | solution.py:172
  120.2 1.4 collective-permute-start.5
  121.6 8.8 %collective-permute-start.7 = (f32[2,2,256,512]{3,2,1,0:T(8,128)}, f32[2,2,256,512]{3,2,1,0:T(8,128)}, u32[]{:S(2)}, u32[]{:S(2)}) collective-permute-start(f32[2,2,256,512]{3,2,1,0:T(8,128)} %get-tuple-element.34), channel_id=1, source_target_pairs={{0,8},{8,16},{16,24},{1,9},{9,17},{17,25},{2,10},{10,18},{18,26},{... | collective-permute-start | bytes 6291464 | tf_op jit(solution)/shard_map/ppermute | solution.py:22
  130.4 2.4 add_dynamic-update-slice_fusion
  132.8 29.4 %collective-permute-start.6 = (f32[2,2,384,256]{3,2,1,0:T(8,128)}, f32[2,2,384,256]{3,2,1,0:T(8,128)}, u32[]{:S(2)}, u32[]{:S(2)}) collective-permute-start(f32[2,2,384,256]{3,2,1,0:T(8,128)} %add_dynamic-update-slice_fusion), channel_id=1, source_target_pairs={{0,1},{1,2},{2,3},{3,4},{4,5},{5,6},{6,7},{8,9},{9,10},{10,11},{11... | collective-permute-start | bytes 4718600 | tf_op jit(solution)/shard_map/ppermute | solution.py:22
  162.5 2.0 copy-done.2
  164.5 1.9 shard_map.96.light
  166.4 28.2 %collective-permute-done.6.left = f32[2,2,384,256]{3,2,1,0:T(8,128)} collective-permute-done((f32[2,2,384,256]{3,2,1,0:T(8,128)}, f32[2,2,384,256]{3,2,1,0:T(8,128)}, u32[]{:S(2)}, u32[]{:S(2)}) %collective-permute-start.6) | collective-permute-done | bytes 1572896 | tf_op jit(solution)/shard_map/ppermute | solution.py:22
  194.5 4.6 %shard_map.97 = f32[2,2,384,512]{3,2,1,0:T(8,128)} custom-call(f32[2,2,384,512]{3,2,1,0:T(8,128)S(1)} %copy-done.1, f32[2,2,384,512]{3,2,1,0:T(8,128)S(1)} %copy-done.4, f32[2,2,384,256]{3,2,1,0:T(8,128)} %collective-permute-done.6.left, f32[2,2,256,512]{3,2,1,0:T(8,128)} %collective-permute-done.7.above, f32[384,512]{1,0:T(8,128)S(1)} %shard_map.96.light), custom_call_target="tpu_custom_call" | custom-call | flops 4000000 | bytes 14000000 | tf_op jit(solution)/shard_map/pallas_call | solution.py:246
  199.2 111.7 %all-reduce.2.cloned.1.call-done = f32[6,2,256,256]{3,2,1,0:T(8,128)} async-done(((f32[6,2,256,256]{3,2,1,0:T(8,128)}), f32[6,2,256,256]{3,2,1,0:T(8,128)}) %all-reduce.2.cloned.1.call-update) | async-done | bytes 3145744 | tf_op jit(solution)/shard_map/psum | solution.py:287
  310.9 3.3 %multiply_reduce_fusion = f32[]{:T(128)} fusion(f32[6,2,256,256]{3,2,1,0:T(8,128)} %all-reduce.2.cloned.1.call-done), kind=kLoop, calls=%fused_computation.1 | loop fusion | flops 1572863 | bytes 3145732 | tf_op jit(solution)/shard_map/reduce_sum | solution.py:294
  314.9 4.0 %divide_subtract_fusion = f32[6,2,256,256]{3,2,1,0:T(8,128)} fusion(f32[6,2,256,256]{3,2,1,0:T(8,128)S(1)} %copy-done.3, f32[6,2,256,256]{3,2,1,0:T(8,128)} %all-reduce.2.cloned.1.call-done, f32[]{:T(128)S(6)} %sqrt.3), kind=kLoop, calls=%fused_computation | loop fusion | flops 2359296 | bytes 9437188 | tf_op jit(solution)/shard_map/sub | solution.py:295
  (33 shorter events, 1.1 us)
Async XLA Ops:
  7.2 3.0 copy-start
  7.2 303.7 %all-reduce.2.cloned.1.call-start = ((), (), s32[]{:S(2)}) async-start(), calls=%async_computation | async-start | bytes 6291456 | tf_op jit(solution)/shard_map/psum | solution.py:287
  8.9 41.8 %copy-start.6 = (s32[3,2]{0,1:T(2,128)S(1)}, s32[3,2]{0,1:T(2,128)}, u32[]{:S(2)}) copy-start(s32[3,2]{0,1:T(2,128)} %param.12) | copy-start | bytes 76
  8.9 39.2 %collective-permute-start = (f32[2,2,384,256]{3,2,1,0:T(8,128)S(1)}, f32[2,2,384,256]{3,2,1,0:T(8,128)S(1)}, u32[]{:S(2)}, u32[]{:S(2)}) collective-permute-start(f32[2,2,384,256]{3,2,1,0:T(8,128)S(1)} %slice.38), channel_id=1, source_target_pairs={{1,0},{2,1},{3,2},{4,3},{5,4},{6,5},{7,6},{9,8},{10,9},{11,10},{12... | collective-permute-start | bytes 4718600 | tf_op jit(solution)/shard_map/ppermute | solution.py:22
  11.7 48.9 %collective-permute-start.1 = (f32[2,2,256,512]{3,2,1,0:T(8,128)}, f32[2,2,256,512]{3,2,1,0:T(8,128)}, u32[]{:S(2)}, u32[]{:S(2)}) collective-permute-start(f32[2,2,256,512]{3,2,1,0:T(8,128)} %slice.39), channel_id=1, source_target_pairs={{8,0},{16,8},{24,16},{9,1},{17,9},{25,17},{10,2},{18,10},{26,18},{... | collective-permute-start | bytes 6291464 | tf_op jit(solution)/shard_map/ppermute | solution.py:22
  48.1 1.2 copy-start.5
  49.4 11.2 %collective-permute-start.2 = (f32[2,2,256,256]{3,2,1,0:T(8,128)S(1)}, f32[2,2,256,256]{3,2,1,0:T(8,128)S(1)}, u32[]{:S(2)}, u32[]{:S(2)}) collective-permute-start(f32[2,2,256,256]{3,2,1,0:T(8,128)S(1)} %slice.42), channel_id=1, source_target_pairs={{8,0},{16,8},{24,16},{9,1},{17,9},{25,17},{10,2},{18,10},{26,18},{... | collective-permute-start | bytes 3145736 | tf_op jit(solution)/shard_map/ppermute | solution.py:22
  51.6 5.8 %collective-permute-start.3 = (s32[7]{0:T(128)S(1)}, s32[7]{0:T(128)S(1)}, u32[]{:S(2)}, u32[]{:S(2)}) collective-permute-start(s32[7]{0:T(128)S(1)} %pad_add_fusion.1), channel_id=1, source_target_pairs={{0,1},{1,2},{2,3},{3,4},{4,5},{5,6},{6,7},{8,9},{9,10},{10,11},{11... | collective-permute-start | bytes 92 | tf_op jit(solution)/shard_map/ppermute | solution.py:22
  57.5 3.0 collective-permute-start.4
  60.6 1.0 copy-start.7
  120.2 10.2 %collective-permute-start.5 = (f32[2,2,256,256]{3,2,1,0:T(8,128)}, f32[2,2,256,256]{3,2,1,0:T(8,128)S(1)}, u32[]{:S(2)}, u32[]{:S(2)}) collective-permute-start(f32[2,2,256,256]{3,2,1,0:T(8,128)} %get-tuple-element.33), channel_id=1, source_target_pairs={{0,8},{8,16},{16,24},{1,9},{9,17},{17,25},{2,10},{10,18},{18,26},{... | collective-permute-start | bytes 3145736 | tf_op jit(solution)/shard_map/ppermute | solution.py:22
  121.6 44.8 %collective-permute-start.7 = (f32[2,2,256,512]{3,2,1,0:T(8,128)}, f32[2,2,256,512]{3,2,1,0:T(8,128)}, u32[]{:S(2)}, u32[]{:S(2)}) collective-permute-start(f32[2,2,256,512]{3,2,1,0:T(8,128)} %get-tuple-element.34), channel_id=1, source_target_pairs={{0,8},{8,16},{16,24},{1,9},{9,17},{17,25},{2,10},{10,18},{18,26},{... | collective-permute-start | bytes 6291464 | tf_op jit(solution)/shard_map/ppermute | solution.py:22
  132.8 61.8 %collective-permute-start.6 = (f32[2,2,384,256]{3,2,1,0:T(8,128)}, f32[2,2,384,256]{3,2,1,0:T(8,128)}, u32[]{:S(2)}, u32[]{:S(2)}) collective-permute-start(f32[2,2,384,256]{3,2,1,0:T(8,128)} %add_dynamic-update-slice_fusion), channel_id=1, source_target_pairs={{0,1},{1,2},{2,3},{3,4},{4,5},{5,6},{6,7},{8,9},{9,10},{10,11},{11... | collective-permute-start | bytes 4718600 | tf_op jit(solution)/shard_map/ppermute | solution.py:22
  162.2 32.4 %copy-start.1 = (f32[2,2,384,512]{3,2,1,0:T(8,128)S(1)}, f32[2,2,384,512]{3,2,1,0:T(8,128)}, u32[]{:S(2)}) copy-start(f32[2,2,384,512]{3,2,1,0:T(8,128)} %tile.22) | copy-start | bytes 9437188
  162.5 2.0 copy-start.2
  164.5 30.1 %copy-start.4 = (f32[2,2,384,512]{3,2,1,0:T(8,128)S(1)}, f32[2,2,384,512]{3,2,1,0:T(8,128)}, u32[]{:S(2)}) copy-start(f32[2,2,384,512]{3,2,1,0:T(8,128)} %get-tuple-element.31.grad) | copy-start | bytes 9437188
  199.1 115.7 %copy-start.3 = (f32[6,2,256,256]{3,2,1,0:T(8,128)S(1)}, f32[6,2,256,256]{3,2,1,0:T(8,128)}, u32[]{:S(2)}) copy-start(f32[6,2,256,256]{3,2,1,0:T(8,128)} %probe.3) | copy-start | bytes 9437188
Sparse Core Ops, SparseCore 0:
  162.3 148.5 all-reduce.1
